TPU v7x, 512 devices: a whole 4x8x8 slice. The times are simulated.
512 devices in a mesh: dp: 16 (over y, core), mp: 32 (over x, z).
Axes of the slice: x: 4, y: 8, z: 8, core: 2. Of those that a mesh axis runs over, the one named last changes fastest.
Arguments:
- grad_partials: bfloat16 [16, 224, 512, 512], P('dp', 'mp')
- owner_lists: int32 [224], replicated, may hold values from 0 to 223, as said below
- owner_offsets: int32 [33], replicated, may hold values from 0 to 224, as said below
- left_roots: bfloat16 [32, 16, 512, 512], P('mp', 'dp')
- right_roots: bfloat16 [32, 16, 512, 512], P('mp', 'dp')
Outputs:
- update: bfloat16 [224, 512, 512], P('mp', 'dp')
Inputs may be any that keep to these rules, and one draw needn't show every extreme that they name: `owner_lists`: a permutation of the block numbers; no owner column owns two blocks of one mp shard (blocks j * 7 to j * 7 + 6). `owner_offsets`: begins with 0, ends with 224, never falls; every owner column owns 1 to 16 blocks, and some column exactly 16.
All inputs are finite; a program needn't handle non-finite values.
Results may differ from a plain program's by a relative error of at most 0.025.
Values may be sent and summed in bfloat16 or wider, within the bound.
A program may use at most 64 MiB of HBM per device.

v0:
```python
import jax
import jax.numpy as jnp
from jax import lax
from jax.sharding import PartitionSpec as P

epsilon = 1e-06
max_rms = 1.0


def shards(grad_partials, owner_lists, owner_offsets, left_roots, right_roots):
    dp_count = lax.axis_size("dp")
    mp_count = lax.axis_size("mp")
    mp_index = lax.axis_index("mp")
    partial_blocks = grad_partials[0]
    per_shard = partial_blocks.shape[0]
    block_width = partial_blocks.shape[2]
    blocks_all = owner_lists.shape[0]
    cells = blocks_all * block_width * block_width
    summed = lax.psum_scatter(
        partial_blocks.astype(jnp.float32).astype(jnp.bfloat16),
        "dp",
        scatter_dimension=1,
        tiled=True,
    )
    slab_f = summed.astype(jnp.float32)
    square_total = lax.psum(jnp.sum(slab_f * slab_f), ("dp", "mp"))
    positions = jnp.arange(blocks_all, dtype=jnp.int32)
    column_of_pos = jnp.sum(
        (owner_offsets[1:][None, :] <= positions[:, None]).astype(jnp.int32), axis=1
    )
    own_blocks = mp_index * per_shard + jnp.arange(per_shard, dtype=jnp.int32)
    matches = owner_lists[None, :] == own_blocks[:, None]
    home_column = jnp.sum(jnp.where(matches, column_of_pos[None, :], 0), axis=1)
    column_ids = jnp.arange(mp_count, dtype=jnp.int32)
    column_pick = (home_column[None, :] == column_ids[:, None]).astype(jnp.bfloat16)
    list_start = owner_offsets[mp_index]
    list_count = owner_offsets[mp_index + 1] - list_start
    slot_ids = jnp.arange(dp_count, dtype=jnp.int32)
    slot_match = positions[None, :] == (list_start + slot_ids)[:, None]
    slot_block = jnp.sum(jnp.where(slot_match, owner_lists[None, :], 0), axis=1)
    slot_live = slot_ids < list_count
    shard_pick = (
        ((slot_block // per_shard)[:, None] == column_ids[None, :]) & slot_live[:, None]
    ).astype(jnp.bfloat16)
    block_ids = jnp.arange(blocks_all, dtype=jnp.int32)
    block_pick = ((slot_block[:, None] == block_ids[None, :]) & slot_live[:, None]).astype(
        jnp.bfloat16
    )
    ordered = jnp.einsum(
        "kb,bsc->ksc",
        block_pick,
        lax.all_gather(summed, "mp", axis=0, tiled=True),
        preferred_element_type=jnp.float32,
    ).astype(jnp.bfloat16)
    whole_block = lax.all_to_all(ordered, "dp", split_axis=0, concat_axis=1, tiled=True)[0]
    right_prod = jnp.dot(whole_block, right_roots[0, 0], preferred_element_type=jnp.float32).astype(
        jnp.bfloat16
    )
    precond = jnp.dot(left_roots[0, 0], right_prod, preferred_element_type=jnp.float32)
    block_f = whole_block.astype(jnp.float32)
    block_sq = jnp.sum(block_f * block_f)
    area = block_width * block_width
    graft_scale = jnp.sqrt(block_sq / area + epsilon) / jnp.sqrt(
        jnp.sum(precond * precond) / area + epsilon
    )
    clip_factor = max_rms / jnp.sqrt(square_total / cells + epsilon)
    finished = (clip_factor * graft_scale * precond).astype(jnp.bfloat16)
    returned_rows = lax.all_to_all(finished[None], "dp", split_axis=1, concat_axis=0, tiled=True)
    outgoing_home = jnp.einsum(
        "km,ksc->msc", shard_pick, returned_rows, preferred_element_type=jnp.float32
    ).astype(jnp.bfloat16)
    arrived_home = lax.all_to_all(outgoing_home, "mp", split_axis=0, concat_axis=0, tiled=True)
    update = jnp.einsum(
        "mr,msc->rsc", column_pick, arrived_home, preferred_element_type=jnp.float32
    )
    return update.astype(jnp.bfloat16)


def solution(mesh):
    return jax.shard_map(
        shards,
        mesh=mesh,
        in_specs=(
            P("dp", "mp", None, None),
            P(),
            P(),
            P("mp", "dp", None, None),
            P("mp", "dp", None, None),
        ),
        out_specs=P("mp", "dp", None),
        check_vma=False,
    )
```

profile of v0, /device:TPU:1, one launch (start us, length us, event | category | flops | bytes accessed | tf_op | source)
XLA Modules:
  0.0 382.2 jit_solution(10315294444294758624)
XLA Ops:
  6.5 0.0 copy-start
  6.5 0.0 copy-start.4
  6.5 0.0 reduce-scatter.2.cloned.1.call-start
  6.5 0.7 reduce-scatter.2.cloned.1.call-update
  7.3 0.0 all-gather.2.cloned.1.call-start
  7.3 70.7 %reduce-scatter.2.cloned.1.call-done = bf16[7,32,512]{2,1,0:T(8,128)(2,1)} async-done(((bf16[7,512,512]{2,1,0:T(8,128)(2,1)}), bf16[7,32,512]{2,1,0:T(8,128)(2,1)}) %reduce-scatter.2.cloned.1.call-update) | async-done | bytes 229392 | tf_op jit(solution)/shard_map/reduce_scatter | solution.py:19
  78.0 0.0 copy-start.1
  78.0 0.0 all-gather.2.cloned.1.call-update
  78.0 1.4 fusion.25
  80.7 0.7 iota_add_fusion
  81.5 0.9 select_reduce_fusion
  82.3 99.0 %all-gather.2.cloned.1.call-done = bf16[224,32,512]{2,1,0:T(8,128)(2,1)} async-done(((bf16[7,32,512]{2,1,0:T(8,128)(2,1)}), bf16[224,32,512]{2,1,0:T(8,128)(2,1)}) %all-gather.2.cloned.1.call-update) | async-done | bytes 7340048 | tf_op jit(solution)/shard_map/all_gather | solution.py:52
  181.3 10.8 %fusion.2 = bf16[16,32,512]{2,0,1:T(8,128)(2,1)S(1)} fusion(bf16[224,32,512]{2,1,0:T(8,128)(2,1)} %all-gather.2.cloned.1.call-done, s32[16]{0:T(128)S(1)} %select_reduce_fusion, pred[16]{0:T(512)(128)(4,1)S(1)} %iota_compare_fusion.5), kind=kOutput, calls=%fused_computation.3 | convolution fusion | flops 117709824 | bytes 7864400 | tf_op jit(solution)/shard_map/kb,bsc->ksc/dot_general | solution.py:49
  192.1 1.1 copy.20
  193.2 7.8 %all-to-all-start = ((bf16[16,32,512]{2,1,0:T(8,128)(2,1)}), bf16[16,32,512]{2,1,0:T(8,128)(2,1)S(1)}, u32[]{:S(2)}, u32[]{:S(2)}) async-start(bf16[16,32,512]{2,1,0:T(8,128)(2,1)} %copy.20), calls=%async_computation.1 | async-start | bytes 1048576 | tf_op jit(solution)/shard_map/all_to_all | solution.py:55
  201.0 0.0 copy-done.1
  201.0 0.7 multiply_reduce_fusion.2
  201.7 101.0 %psum.7 = f32[]{:T(128)} all-reduce(f32[]{:T(128)} %multiply_reduce_fusion.2), channel_id=1, replica_groups=mesh['dp'=16,'mp'=32] {'dp','mp'}, use_global_device_ids=true, to_apply=%region_5.6 | all-reduce | flops 1 | bytes 8 | tf_op jit(solution)/shard_map/psum | solution.py:26
  303.4 0.0 all-to-all-done
  303.4 0.9 multiply_reduce_fusion.1
  305.0 0.0 copy-done
  305.0 0.0 copy-done.4
  305.0 1.5 multiply_reduce_fusion
  307.3 0.1 fusion.7
  307.4 0.0 copy-start.3
  307.4 0.0 copy-start.2
  307.4 0.9 copy.21
  308.3 0.5 broadcast.48
  308.8 3.8 reduce.2
  312.6 1.2 reshape.37
  313.8 7.2 %all-to-all-start.1 = ((bf16[16,2,8192]{2,1,0:T(2,128)(2,1)}), bf16[16,2,8192]{2,1,0:T(2,128)(2,1)S(1)}, u32[]{:S(2)}, u32[]{:S(2)}) async-start(bf16[16,2,8192]{2,1,0:T(2,128)(2,1)} %reshape.37), calls=%async_computation.2 | async-start | bytes 1048576 | tf_op jit(solution)/shard_map/all_to_all | solution.py:68
  321.0 17.3 %all-to-all-done.1 = bf16[16,2,8192]{2,1,0:T(2,128)(2,1)S(1)} async-done(((bf16[16,2,8192]{2,1,0:T(2,128)(2,1)}), bf16[16,2,8192]{2,1,0:T(2,128)(2,1)S(1)}, u32[]{:S(2)}, u32[]{:S(2)}) %all-to-all-start.1) | async-done | bytes 524320 | tf_op jit(solution)/shard_map/all_to_all | solution.py:68
  338.3 0.5 reshape.38
  338.8 0.1 copy.26
  338.9 0.6 convolution_convert_fusion
  339.5 1.6 copy.23
  341.1 4.7 %all-to-all-start.2 = ((bf16[32,32,512]{2,1,0:T(8,128)(2,1)}), bf16[32,32,512]{2,1,0:T(8,128)(2,1)S(1)}, u32[]{:S(2)}, u32[]{:S(2)}) async-start(bf16[32,32,512]{2,1,0:T(8,128)(2,1)} %copy.23), calls=%async_computation.3 | async-start | bytes 2097152 | tf_op jit(solution)/shard_map/all_to_all | solution.py:72
  345.8 0.0 copy-done.3
  345.9 0.1 slice.3
  345.9 0.1 convert_reduce_fusion
  346.0 0.0 copy-done.2
  346.0 0.2 select_reduce_fusion.1
  346.2 27.7 %all-to-all-done.2 = bf16[32,32,512]{2,1,0:T(8,128)(2,1)S(1)} async-done(((bf16[32,32,512]{2,1,0:T(8,128)(2,1)}), bf16[32,32,512]{2,1,0:T(8,128)(2,1)S(1)}, u32[]{:S(2)}, u32[]{:S(2)}) %all-to-all-start.2) | async-done | bytes 1048608 | tf_op jit(solution)/shard_map/all_to_all | solution.py:72
  373.9 0.7 convolution_convert_fusion.2
  374.6 0.8 copy.25
  (3 shorter events, 0.0 us)
Async XLA Ops:
  6.5 298.5 %copy-start = (bf16[1,1,512,512]{3,2,1,0:T(8,128)(2,1)S(1)}, bf16[1,1,512,512]{3,2,1,0:T(8,128)(2,1)}, u32[]{:S(2)}) copy-start(bf16[1,1,512,512]{3,2,1,0:T(8,128)(2,1)} %param.8) | copy-start | bytes 1572868
  6.5 298.5 %copy-start.4 = (bf16[1,1,512,512]{3,2,1,0:T(8,128)(2,1)S(1)}, bf16[1,1,512,512]{3,2,1,0:T(8,128)(2,1)}, u32[]{:S(2)}) copy-start(bf16[1,1,512,512]{3,2,1,0:T(8,128)(2,1)} %param.9) | copy-start | bytes 1572868
  6.5 71.4 %reduce-scatter.2.cloned.1.call-start = ((), (), s32[]{:S(2)}) async-start(), calls=%async_computation.4 | async-start | bytes 3899392 | tf_op jit(solution)/shard_map/reduce_scatter | solution.py:19
  7.3 174.0 %all-gather.2.cloned.1.call-start = ((), (), s32[]{:S(2)}) async-start(), calls=%async_computation.5 | async-start | bytes 7569408 | tf_op jit(solution)/shard_map/all_gather | solution.py:52
  78.0 123.0 %copy-start.1 = (bf16[7,32,512]{2,1,0:T(8,128)(2,1)S(1)}, bf16[7,32,512]{2,1,0:T(8,128)(2,1)}, u32[]{:S(2)}) copy-start(bf16[7,32,512]{2,1,0:T(8,128)(2,1)} %reduce-scatter.2.cloned.1.call-done) | copy-start | bytes 688132
  193.2 110.3 %all-to-all-start = ((bf16[16,32,512]{2,1,0:T(8,128)(2,1)}), bf16[16,32,512]{2,1,0:T(8,128)(2,1)S(1)}, u32[]{:S(2)}, u32[]{:S(2)}) async-start(bf16[16,32,512]{2,1,0:T(8,128)(2,1)} %copy.20), calls=%async_computation.1 | async-start | bytes 1048576 | tf_op jit(solution)/shard_map/all_to_all | solution.py:55
  307.4 38.5 %copy-start.3 = (s32[33]{0:T(128)S(1)}, s32[33]{0:T(128)}, u32[]{:S(2)}) copy-start(s32[33]{0:T(128)} %param.7) | copy-start | bytes 400
  307.4 38.6 %copy-start.2 = (s32[224]{0:T(256)S(1)}, s32[224]{0:T(256)}, u32[]{:S(2)}) copy-start(s32[224]{0:T(256)} %param.6) | copy-start | bytes 2692
  313.8 24.5 %all-to-all-start.1 = ((bf16[16,2,8192]{2,1,0:T(2,128)(2,1)}), bf16[16,2,8192]{2,1,0:T(2,128)(2,1)S(1)}, u32[]{:S(2)}, u32[]{:S(2)}) async-start(bf16[16,2,8192]{2,1,0:T(2,128)(2,1)} %reshape.37), calls=%async_computation.2 | async-start | bytes 1048576 | tf_op jit(solution)/shard_map/all_to_all | solution.py:68
  341.1 32.8 %all-to-all-start.2 = ((bf16[32,32,512]{2,1,0:T(8,128)(2,1)}), bf16[32,32,512]{2,1,0:T(8,128)(2,1)S(1)}, u32[]{:S(2)}, u32[]{:S(2)}) async-start(bf16[32,32,512]{2,1,0:T(8,128)(2,1)} %copy.23), calls=%async_computation.3 | async-start | bytes 2097152 | tf_op jit(solution)/shard_map/all_to_all | solution.py:72
Sparse Core Ops, SparseCore 0:
  10.2 67.7 reduce-scatter.1
  81.1 100.1 all-gather.1
where the time goes:
time: 383 us; the launch traced here: 382 us
  waiting for transfers between devices  215 us (56%)
  blocking collectives  101 us (26%)
  starting transfers between devices  19.8 us (5%)
  between operations  17 us (4%)
  matrix products  13.6 us (4%)
  local copies, waits for them, and re-layouts  8.13 us (2%)
  other arithmetic  7.38 us (2%)
    psum x1, blocking collectives, shards(): square_total = lax.psum(jnp.sum(slab_f * slab_f), ('dp', 'mp'))  101 us
    all_gather x1, waiting for transfers between devices, shards(): lax.all_gather(summed, 'mp', axis=0, tiled=True)  99 us
    reduce_scatter x1, waiting for transfers between devices, shards(): lax.psum_scatter(partial_blocks.astype(jnp.float32).astype(jnp.bfloat16),...  70.7 us
    all_to_all x1, waiting for transfers between devices, shards(): lax.all_to_all(outgoing_home, 'mp', split_axis=0, concat_axis=0, tiled=True)  27.7 us
    all_to_all x1, waiting for transfers between devices, shards(): lax.all_to_all(finished[None], 'dp', split_axis=1, concat_axis=0, tiled=T...  17.3 us
    dot_general x1, matrix products, shards(): jnp.einsum('kb,bsc->ksc', block_pick, lax.all_gather(summed, 'mp', axis=0...  10.8 us
    all_to_all x1, starting transfers between devices, shards(): lax.all_to_all(ordered, 'dp', split_axis=0, concat_axis=1, tiled=True)[0]  7.83 us
  transfers between devices with their start and end apart: 5, of which 4 were waited for; matrix products, arithmetic and copies ran while one was open for 1% of the time, Pallas kernels for 0%

commit v1 on v0

v1 whole, which is shorter than its diff:
```python
import functools

import jax
import jax.numpy as jnp
from jax import lax
from jax.experimental import pallas as pl
from jax.experimental.pallas import tpu as pltpu
from jax.sharding import PartitionSpec as P

MESH = pl.DeviceIdType.MESH
F32 = jnp.float32
BF16 = jnp.bfloat16

epsilon = 1e-06
max_rms = 1.0

CHUNKS = 2
NY, NX, NZ = 8, 4, 8
SLAB = 32
HALF = SLAB // 2

T_FWD = 0
T_SLOT = 32
T_RET = 48
T_HX = 80
T_MINE = 136
T_SIZE = 192


def routing_tables(owner_lists, owner_offsets, per_shard):
    blocks = owner_lists.shape[0]
    mp = lax.axis_index("mp")
    x, z = mp // NZ, mp % NZ
    positions = jnp.arange(blocks, dtype=jnp.int32)
    column_of_pos = jnp.sum(
        (owner_offsets[1:][None, :] <= positions[:, None]).astype(jnp.int32), axis=1
    )
    line = NZ * per_shard
    line_blocks = x * line + jnp.arange(line, dtype=jnp.int32)
    matches = owner_lists[None, :] == line_blocks[:, None]
    home = jnp.sum(jnp.where(matches, column_of_pos[None, :], 0), axis=1).reshape(NZ, per_shard)
    home_x, mine = home // NZ, (home % NZ == z).astype(jnp.int32)
    to_x = jnp.arange(NX, dtype=jnp.int32)
    ids = jnp.arange(per_shard, dtype=jnp.int32)
    picked = home[:, None, :] == (to_x * NZ + z)[None, :, None]
    forward = jnp.sum(jnp.where(picked, ids[None, None, :], 0), axis=2)
    start = owner_offsets[mp]
    count = owner_offsets[mp + 1] - start
    slots = jnp.arange(2 * NY, dtype=jnp.int32)
    at = (start + slots)[:, None] == positions[None, :]
    block = jnp.sum(jnp.where(at, owner_lists[None, :], 0), axis=1)
    shard = block // per_shard
    delta = (shard % NZ - z + NZ) % NZ
    place = jnp.where(
        delta == 0, 0, jnp.where(delta < 4, 2 * delta - 1, jnp.where(delta == 4, 7, 2 * (NZ - delta)))
    )
    slot_place = (shard // NZ) * NZ + place
    shards_all = jnp.arange(NX * NZ, dtype=jnp.int32)
    owned = (shard[None, :] == shards_all[:, None]) & (slots < count)[None, :]
    back = jnp.sum(jnp.where(owned, slots[None, :], 0), axis=1)
    parts = [forward.reshape(-1), slot_place, back, home_x.reshape(-1), mine.reshape(-1)]
    return jnp.concatenate(parts).astype(jnp.int32)


def kernel(
    nc,
    cells,
    tab,
    g,
    left,
    right,
    out,
    own,
    other,
    red,
    slab,
    zin,
    zfar,
    xsend,
    arrived,
    csend,
    block,
    done,
    rows,
    esend,
    ein,
    emix,
    ered,
    lv,
    rv,
    acc,
    sq,
    sq_d,
    sq_x,
    sq_z,
    sem_in,
    core_s,
    core_r,
    ra_s,
    ra_r,
    rb_s,
    rb_r,
    xb_s,
    xb_r,
    c_s,
    c_r,
    d_s,
    d_r,
    xe_s,
    xe_r,
    re_s,
    re_r,
    qd_s,
    qd_r,
    qx_s,
    qx_r,
    qz_s,
    qz_r,
):
    per_shard = g.shape[0]
    width = g.shape[-1] // nc
    edge = g.shape[-1]
    area = edge * edge
    n_dp = 2 * NY
    dp = lax.axis_index("dp")
    mp = lax.axis_index("mp")
    y, core = dp // 2, dp % 2
    x, z = mp // NZ, mp % NZ
    mate = y * 2 + (1 - core)
    y_to = [((y + NY - 1) % NY) * 2 + core, ((y + 1) % NY) * 2 + core]
    z_to = [x * NZ + (z + NZ - 1) % NZ, x * NZ + (z + 1) % NZ]

    def x_to(j):
        return ((x + j) % NX) * NZ + z

    def cols(c):
        return pl.ds(c * width, width)

    sent = []

    def send(src, dst, ss, rs, dev):
        copy = pltpu.make_async_remote_copy(
            src_ref=src, dst_ref=dst, send_sem=ss, recv_sem=rs, device_id=dev, device_id_type=MESH
        )
        copy.start()
        sent.append(copy)

    def received(dst, rs, ss):
        pltpu.make_async_remote_copy(
            src_ref=dst, dst_ref=dst, send_sem=ss, recv_sem=rs, device_id={"dp": mate}, device_id_type=MESH
        ).wait_recv()

    loads = []
    for c in range(nc):
        load = pltpu.make_async_copy(g.at[:, :, core, :, cols(c)], own.at[c], sem_in.at[c])
        load.start()
        loads.append(load)
    load_r = pltpu.make_async_copy(right, rv, sem_in.at[nc])
    load_r.start()
    load_l = pltpu.make_async_copy(left, lv, sem_in.at[nc + 1])
    load_l.start()

    barrier = pltpu.get_barrier_semaphore()

    @pl.loop(1, n_dp)
    def _(o):
        pl.semaphore_signal(barrier, inc=1, device_id={"dp": (dp + o) % n_dp}, device_id_type=MESH)

    @pl.loop(1, NX)
    def _(o):
        pl.semaphore_signal(barrier, inc=1, device_id={"mp": ((x + o) % NX) * NZ + z}, device_id_type=MESH)

    @pl.loop(1, NZ)
    def _(o):
        pl.semaphore_signal(barrier, inc=1, device_id={"mp": x * NZ + (z + o) % NZ}, device_id_type=MESH)

    pl.semaphore_wait(barrier, n_dp + NX + NZ - 3)

    for c in range(nc):
        send(g.at[:, :, 1 - core, :, cols(c)], other.at[c], core_s.at[c], core_r.at[c], {"dp": mate})

    lo, hi = pl.ds(0, HALF), pl.ds(HALF, HALF)
    part = [lo, hi]

    def pair(c, t, r):
        return own[c, :, t, r].astype(F32) + other[c, :, t, r].astype(F32)

    everything = pl.ds(0, SLAB)

    def a0(c):
        loads[c].wait()
        received(other.at[c], core_r.at[c], core_s.at[c])
        t = (y + 4) % NY
        own[c, :, t] = pair(c, t, everything).astype(BF16)
        for way in range(2):
            send(
                own.at[c, :, t, part[way]],
                red.at[c, way, 0, :, part[way]],
                ra_s.at[c, way, 0],
                ra_r.at[c, way, 0],
                {"dp": y_to[way]},
            )

    def a_mid(c, s):
        for way in range(2):
            t = (y + NY + (s - 4 if way == 0 else 4 - s)) % NY
            if s == 1:
                here, rest = part[way], part[1 - way]
                received(red.at[c, way, 0, :, here], ra_r.at[c, way, 0], ra_s.at[c, way, 0])
                own[c, :, t, here] = (pair(c, t, here) + red[c, way, 0, :, here].astype(F32)).astype(BF16)
                own[c, :, t, rest] = pair(c, t, rest).astype(BF16)
            else:
                received(red.at[c, way, s - 1], ra_r.at[c, way, s - 1], ra_s.at[c, way, s - 1])
                own[c, :, t] = (pair(c, t, everything) + red[c, way, s - 1].astype(F32)).astype(BF16)
            send(own.at[c, :, t], red.at[c, way, s], ra_s.at[c, way, s], ra_r.at[c, way, s], {"dp": y_to[way]})

    def squares(v):
        v = (v * v).reshape(-1, 8, v.shape[-1])
        v = jnp.sum(v, axis=0)
        return sum(v[:, i * 128 : (i + 1) * 128] for i in range(v.shape[-1] // 128))

    def a4(c):
        total = pair(c, y, everything)
        for way in range(2):
            received(red.at[c, way, 3], ra_r.at[c, way, 3], ra_s.at[c, way, 3])
            total += red[c, way, 3].astype(F32)
        total = total.astype(BF16)
        slab[c] = total
        for way in range(2):
            send(slab.at[c], zin[c][way][0], rb_s.at[c, way, 0], rb_r.at[c, way, 0], {"mp": z_to[way]})
        part_sq = squares(total.astype(F32))
        sq[0] = part_sq if c == 0 else sq[0] + part_sq
        pick(c, slab.at[c], z, 0)

    def pick(c, src, zs, place):
        for j in range(NX):
            chosen = src[tab[T_FWD + zs * NX + (x + j) % NX]]
            if j == 0:
                arrived[c][x * NZ + place] = chosen
            else:
                xsend[c, j - 1, place] = chosen

    groups = [(0, 3), (3, 2), (5, 2), (7, 1)]

    def x_send(c, n):
        first, size = groups[n]
        for j in range(1, NX):
            send(
                xsend.at[c, j - 1, pl.ds(first, size)],
                arrived[c].at[pl.ds(x * NZ + first, size)],
                xb_s.at[c, j - 1, n],
                xb_r.at[c, j - 1, n],
                {"mp": x_to(j)},
            )

    def b_mid(c, s):
        for way in range(2):
            received(zin[c][way][s - 1], rb_r.at[c, way, s - 1], rb_s.at[c, way, s - 1])
            if s < 3:
                src, dst = zin[c][way][s - 1], zin[c][way][s]
            else:
                src, dst = zin[c][way][2].at[:, part[way]], zfar[c].at[:, part[way]]
            send(src, dst, rb_s.at[c, way, s], rb_r.at[c, way, s], {"mp": z_to[way]})
        for way in range(2):
            zs = (z + s) % NZ if way == 0 else (z + NZ - s) % NZ
            pick(c, zin[c][way][s - 1], zs, 2 * s - 1 + way)
        x_send(c, s - 1)

    def b4(c):
        for way in range(2):
            received(zfar[c].at[:, part[way]], rb_r.at[c, way, 3], rb_s.at[c, way, 3])
        pick(c, zfar[c], (z + 4) % NZ, 7)
        x_send(c, 3)

    def c0(c):
        for j in range(1, NX):
            for n in range(4):
                first, size = groups[n]
                came = arrived[c].at[pl.ds(((x + NX - j) % NX) * NZ + first, size)]
                received(came, xb_r.at[c, j - 1, n], xb_s.at[c, j - 1, n])
        block[c, dp] = arrived[c][tab[T_SLOT + dp]]

        @pl.loop(1, n_dp)
        def _(o):
            k = (dp + o) % n_dp
            csend[c, k] = arrived[c][tab[T_SLOT + k]]
            pltpu.make_async_remote_copy(
                src_ref=csend.at[c, k],
                dst_ref=block.at[c, dp],
                send_sem=c_s.at[c, o],
                recv_sem=c_r.at[c, o],
                device_id={"dp": k},
                device_id_type=MESH,
            ).start()

    def dp_received(buf, c, rs, ss):
        @pl.loop(1, n_dp)
        def _(o):
            received(buf.at[(dp + n_dp - o) % n_dp], rs.at[c, o], ss.at[c, o])

    def c1(c):
        dp_received(block.at[c], c, c_r, c_s)
        if c == 0:
            load_r.wait()
        rows_c = block[c].reshape(edge, width)
        product = jnp.dot(rows_c, rv[cols(c), :], preferred_element_type=F32)
        acc[...] = product if c == 0 else acc[...] + product
        part_sq = squares(rows_c.astype(F32))
        sq[3] = part_sq if c == 0 else sq[3] + part_sq

    def q0():
        @pl.loop(1, n_dp)
        def _(o):
            pltpu.make_async_remote_copy(
                src_ref=sq.at[0],
                dst_ref=sq_d.at[o],
                send_sem=qd_s.at[o],
                recv_sem=qd_r.at[o],
                device_id={"dp": (dp + o) % n_dp},
                device_id_type=MESH,
            ).start()

    def q1():
        total = sq[0]
        for o in range(1, n_dp):
            received(sq_d.at[o], qd_r.at[o], qd_s.at[o])
            total += sq_d[o]
        sq[1] = total
        for j in range(1, NX):
            send(sq.at[1], sq_x.at[j], qx_s.at[j], qx_r.at[j], {"mp": x_to(j)})

    def q2():
        total = sq[1]
        for j in range(1, NX):
            received(sq_x.at[j], qx_r.at[j], qx_s.at[j])
            total += sq_x[j]
        sq[2] = total
        for o in range(1, NZ):
            send(sq.at[2], sq_z.at[o], qz_s.at[o], qz_r.at[o], {"mp": x * NZ + (z + o) % NZ})

    def q3():
        total = sq[2]
        for o in range(1, NZ):
            received(sq_z.at[o], qz_r.at[o], qz_s.at[o])
            total += sq_z[o]
        return jnp.sum(total, keepdims=True)

    stages = [
        a0,
        functools.partial(a_mid, s=1),
        functools.partial(a_mid, s=2),
        functools.partial(a_mid, s=3),
        a4,
        functools.partial(b_mid, s=1),
        functools.partial(b_mid, s=2),
        functools.partial(b_mid, s=3),
        b4,
        c0,
        c1,
    ]
    for slot in range(len(stages) + nc - 1):
        for c in range(nc):
            n = slot - c
            if 0 <= n < len(stages):
                stages[n](c)
            if c == nc - 1:
                if n == 4:
                    q0()
                if n == 6:
                    q1()
                if n == 8:
                    q2()

    load_l.wait()
    acc[...] = jnp.dot(lv[...], acc[...].astype(BF16), preferred_element_type=F32)
    precond_sq = sum(squares(acc[:, cols(c)]) for c in range(nc))
    graft = jnp.sqrt(jnp.sum(sq[3], keepdims=True) / area + epsilon) / jnp.sqrt(
        jnp.sum(precond_sq, keepdims=True) / area + epsilon
    )
    clip = max_rms / jnp.sqrt(q3() / cells + epsilon)
    scale = clip * graft

    def d0(c):
        done[c] = (scale * acc[:, cols(c)]).astype(BF16).reshape(n_dp, SLAB, width)
        rows[c][dp] = done[c, dp]

        @pl.loop(1, n_dp)
        def _(o):
            k = (dp + o) % n_dp
            pltpu.make_async_remote_copy(
                src_ref=done.at[c, k],
                dst_ref=rows[c].at[dp],
                send_sem=d_s.at[c, o],
                recv_sem=d_r.at[c, o],
                device_id={"dp": k},
                device_id_type=MESH,
            ).start()

    def e0(c):
        dp_received(rows[c], c, d_r, d_s)
        for j in [1, 2, 3, 0]:
            for zs in range(NZ):
                chosen = rows[c][tab[T_RET + ((x + j) % NX) * NZ + zs]]
                if j == 0:
                    ein[c][x, zs] = chosen
                else:
                    esend[c, j - 1, zs] = chosen
            if j:
                send(esend.at[c, j - 1], ein[c].at[x], xe_s.at[c, j - 1], xe_r.at[c, j - 1], {"mp": x_to(j)})

    def merge(c, t, i, r, incoming):
        at = t * per_shard + i
        return jnp.where(tab[T_MINE + at] == 1, ein[c][tab[T_HX + at], t, r], incoming)

    zero_half = jnp.zeros((HALF, width), BF16)
    zero = jnp.zeros((SLAB, width), BF16)

    def e1(c):
        for j in range(1, NX):
            received(ein[c].at[(x + NX - j) % NX], xe_r.at[c, j - 1], xe_s.at[c, j - 1])
        t = (z + 4) % NZ
        for i in range(per_shard):
            emix[c, t, i] = merge(c, t, i, everything, zero)
        for way in range(2):
            send(
                emix.at[c, t, :, part[way]],
                ered.at[c, way, 0, :, part[way]],
                re_s.at[c, way, 0],
                re_r.at[c, way, 0],
                {"mp": z_to[way]},
            )

    def e_mid(c, s):
        for way in range(2):
            t = (z + NZ + (s - 4 if way == 0 else 4 - s)) % NZ
            if s == 1:
                here, rest = part[way], part[1 - way]
                received(ered.at[c, way, 0, :, here], re_r.at[c, way, 0], re_s.at[c, way, 0])
                for i in range(per_shard):
                    emix[c, t, i, here] = merge(c, t, i, here, ered[c, way, 0, i, here])
                    emix[c, t, i, rest] = merge(c, t, i, rest, zero_half)
            else:
                received(ered.at[c, way, s - 1], re_r.at[c, way, s - 1], re_s.at[c, way, s - 1])
                for i in range(per_shard):
                    emix[c, t, i] = merge(c, t, i, everything, ered[c, way, s - 1, i])
            send(emix.at[c, t], ered.at[c, way, s], re_s.at[c, way, s], re_r.at[c, way, s], {"mp": z_to[way]})

    def e5(c):
        for way in range(2):
            received(ered.at[c, way, 3], re_r.at[c, way, 3], re_s.at[c, way, 3])
        for i in range(per_shard):
            out[i, :, cols(c)] = merge(c, z, i, everything, ered[c, 0, 3, i] + ered[c, 1, 3, i])

    for c in range(nc):
        d0(c)
    stages = [
        e0,
        e1,
        functools.partial(e_mid, s=1),
        functools.partial(e_mid, s=2),
        functools.partial(e_mid, s=3),
        e5,
    ]
    for slot in range(len(stages) + nc - 1):
        for c in range(nc):
            if 0 <= slot - c < len(stages):
                stages[slot - c](c)

    for copy in sent:
        copy.wait_send()

    @pl.loop(1, n_dp)
    def _(o):
        for c in range(nc):
            k = (dp + o) % n_dp
            for src, ss, rs in ((csend, c_s, c_r), (done, d_s, d_r)):
                pltpu.make_async_remote_copy(
                    src_ref=src.at[c, k],
                    dst_ref=src.at[c, k],
                    send_sem=ss.at[c, o],
                    recv_sem=rs.at[c, o],
                    device_id={"dp": k},
                    device_id_type=MESH,
                ).wait_send()
        pltpu.make_async_remote_copy(
            src_ref=sq.at[0],
            dst_ref=sq_d.at[o],
            send_sem=qd_s.at[o],
            recv_sem=qd_r.at[o],
            device_id={"dp": (dp + o) % n_dp},
            device_id_type=MESH,
        ).wait_send()


def shards(grad_partials, owner_lists, owner_offsets, left_roots, right_roots):
    _, per_shard, edge, _ = grad_partials.shape
    nc = CHUNKS
    width = edge // nc
    n_dp = 2 * NY
    tables = routing_tables(owner_lists, owner_offsets, per_shard)
    g = grad_partials.reshape(per_shard, NY, 2, SLAB, edge)
    dma = pltpu.SemaphoreType.DMA

    def both(*shape):
        return [dma(shape), dma(shape)]

    anywhere = pl.BlockSpec(memory_space=pl.ANY)
    return pl.pallas_call(
        functools.partial(kernel, nc, owner_lists.shape[0] * edge * edge),
        out_shape=jax.ShapeDtypeStruct((per_shard, SLAB, edge), BF16),
        in_specs=[pl.BlockSpec(memory_space=pltpu.SMEM), anywhere, anywhere, anywhere],
        out_specs=pl.BlockSpec(memory_space=pltpu.VMEM),
        scratch_shapes=[
            pltpu.VMEM((nc, per_shard, NY, SLAB, width), BF16),
            pltpu.VMEM((nc, per_shard, NY, SLAB, width), BF16),
            pltpu.VMEM((nc, 2, 4, per_shard, SLAB, width), BF16),
            pltpu.VMEM((nc, per_shard, SLAB, width), BF16),
            [[[pltpu.VMEM((per_shard, SLAB, width), BF16)] * 3] * 2] * nc,
            [pltpu.VMEM((per_shard, SLAB, width), BF16)] * nc,
            pltpu.VMEM((nc, NX - 1, NZ, SLAB, width), BF16),
            [pltpu.VMEM((NX * NZ, SLAB, width), BF16)] * nc,
            pltpu.VMEM((nc, n_dp, SLAB, width), BF16),
            pltpu.VMEM((nc, n_dp, SLAB, width), BF16),
            pltpu.VMEM((nc, n_dp, SLAB, width), BF16),
            [pltpu.VMEM((n_dp, SLAB, width), BF16)] * nc,
            pltpu.VMEM((nc, NX - 1, NZ, SLAB, width), BF16),
            [pltpu.VMEM((NX, NZ, SLAB, width), BF16)] * nc,
            pltpu.VMEM((nc, NZ, per_shard, SLAB, width), BF16),
            pltpu.VMEM((nc, 2, 4, per_shard, SLAB, width), BF16),
            pltpu.VMEM((edge, edge), BF16),
            pltpu.VMEM((edge, edge), BF16),
            pltpu.VMEM((edge, edge), F32),
            pltpu.VMEM((4, 8, 128), F32),
            pltpu.VMEM((n_dp, 8, 128), F32),
            pltpu.VMEM((NX, 8, 128), F32),
            pltpu.VMEM((NZ, 8, 128), F32),
            dma((nc + 2,)),
            *both(nc),
            *both(nc, 2, 4),
            *both(nc, 2, 4),
            *both(nc, NX - 1, 4),
            *both(nc, n_dp),
            *both(nc, n_dp),
            *both(nc, NX - 1),
            *both(nc, 2, 4),
            *both(n_dp),
            *both(NX),
            *both(NZ),
        ],
        compiler_params=pltpu.CompilerParams(
            collective_id=0, has_side_effects=True, vmem_limit_bytes=48 * 1024 * 1024
        ),
    )(tables, g, left_roots[0, 0], right_roots[0, 0])


def solution(mesh):
    return jax.shard_map(
        shards,
        mesh=mesh,
        in_specs=(
            P("dp", "mp", None, None),
            P(),
            P(),
            P("mp", "dp", None, None),
            P("mp", "dp", None, None),
        ),
        out_specs=P("mp", "dp", None),
        check_vma=False,
    )
```

time: 383 us -> 134 us (0.35)
  waiting for transfers between devices: 215 us -> 0 us
  Pallas kernels: 0 us -> 121 us
  blocking collectives: 101 us -> 0 us
  starting transfers between devices: 19.8 us -> 0 us
  between operations: 17 us -> 1.4 us
  matrix products: 13.6 us -> 0 us
  other arithmetic: 7.38 us -> 2.75 us
    pallas_call x0 -> x1, Pallas kernels: none -> 121 us  [shards(): pl.pallas_call(functools.partial(kernel, nc, owner_lists.shape[0] * edge...]
    psum x1 -> x0, blocking collectives: 101 us -> none  [shards(): square_total = lax.psum(jnp.sum(slab_f * slab_f), ('dp', 'mp'))]
    all_gather x1 -> x0, waiting for transfers between devices: 99 us -> none  [shards(): lax.all_gather(summed, 'mp', axis=0, tiled=True)]
    reduce_scatter x1 -> x0, waiting for transfers between devices: 70.7 us -> none  [shards(): lax.psum_scatter(partial_blocks.astype(jnp.float32).astype(jnp.bfloat16),...]
    all_to_all x3 -> x0, waiting for transfers between devices: 45 us -> none  [the longest x1 27.7 us: shards(): lax.all_to_all(outgoing_home, 'mp', split_axis=0, concat_axis=0, tiled=True)]
    all_to_all x3 -> x0, starting transfers between devices: 19.7 us -> none  [the longest x1 7.83 us: shards(): lax.all_to_all(ordered, 'dp', split_axis=0, concat_axis=1, tiled=True)[0]]
    dot_general x4 -> x0, matrix products: 13.6 us -> none  [the longest x1 10.8 us: shards(): jnp.einsum('kb,bsc->ksc', block_pick, lax.all_gather(summed, 'mp', axis=0...]
  transfers between devices with their start and end apart: 5 -> 0, of which waited for: 4 -> 0; matrix products, arithmetic and copies ran while one was open for 1% -> 0% of each run, Pallas kernels for 0% -> 0%
where the time goes in v1:
time: 134 us; the launch traced here: 133 us
  Pallas kernels  121 us (90%)
  local copies, waits for them, and re-layouts  7.35 us (5%)
  other arithmetic  2.75 us (2%)
  between operations  1.4 us (1%)
    pallas_call x1, Pallas kernels, shards(): pl.pallas_call(functools.partial(kernel, nc, owner_lists.shape[0] * edge...  121 us
    unnamed x7, local copies, waits for them, and re-layouts  4.82 us

profile of v1, /device:TPU:1, one launch (start us, length us, event | category | flops | bytes accessed | tf_op | source)
XLA Modules:
  0.0 132.9 jit_solution(13071804895507821054)
XLA Ops:
  0.0 1.4 %fusion.5 = (s32[1]{0:T(128)}, s32[1]{0:T(128)}) fusion(s32[33]{0:T(128)} %param.7, s32[]{:T(128)S(6)} %select_n.91, s32[]{:T(128)S(6)} %select_n.82), kind=kLoop, calls=%fused_computation.35 | loop fusion | bytes 24 | tf_op jit(solution)/shard_map/dynamic_slice | solution.py:48
  2.7 0.7 iota_add_fusion
  3.4 0.9 select_reduce_fusion.1
  4.3 0.7 slice.3
  5.0 0.1 convert_reduce_fusion
  5.1 0.9 select_reduce_fusion
  6.1 0.1 select_reduce_fusion.3
  6.2 0.1 eq.77
  6.2 0.1 copy.6
  6.3 0.1 select_reduce_fusion.2
  6.4 0.1 copy.7
  6.5 0.1 reshape.40
  6.6 0.1 concatenate.3.tab
  6.7 0.0 copy-start
  6.7 2.0 %copy-done = bf16[1,7,512,512]{3,2,1,0:T(8,128)(2,1)S(1)} copy-done((bf16[1,7,512,512]{3,2,1,0:T(8,128)(2,1)S(1)}, bf16[1,7,512,512]{3,2,1,0:T(8,128)(2,1)}, u32[]{:S(2)}) %copy-start) | copy-done | bytes 3670040
  8.7 0.0 copy-start.1
  8.7 1.0 copy-done.1
  9.8 0.0 copy-start.2
  9.8 1.0 copy-done.2
  10.8 121.4 %shard_map.55 = bf16[7,32,512]{2,1,0:T(8,128)(2,1)S(1)} custom-call(s32[192]{0:T(256)S(1)} %concatenate.3.tab, bf16[7,8,2,32,512]{4,3,2,1,0:T(8,128)(2,1)S(1)} %bitcast.5, bf16[512,512]{1,0:T(8,128)(2,1)S(1)} %bitcast.6, bf16[512,512]{1,0:T(8,128)(2,1)S(1)} %bitcast.7), custom_call_target="tpu_custom_call" | custom-call | tf_op jit(solution)/shard_map/pallas_call | solution.py:508
  132.2 0.7 copy.9
  (6 shorter events, 0.1 us)
Async XLA Ops:
  6.7 2.0 %copy-start = (bf16[1,7,512,512]{3,2,1,0:T(8,128)(2,1)S(1)}, bf16[1,7,512,512]{3,2,1,0:T(8,128)(2,1)}, u32[]{:S(2)}) copy-start(bf16[1,7,512,512]{3,2,1,0:T(8,128)(2,1)} %param.5) | copy-start | bytes 11010052
  8.7 1.0 copy-start.1
  9.8 1.0 copy-start.2

commit v2 on v0

v2 whole, which is shorter than its diff:
```python
import functools

import jax
import jax.numpy as jnp
from jax import lax
from jax.experimental import pallas as pl
from jax.experimental.pallas import tpu as pltpu
from jax.sharding import PartitionSpec as P

MESH = pl.DeviceIdType.MESH
F32 = jnp.float32
BF16 = jnp.bfloat16

epsilon = 1e-06
max_rms = 1.0

CHUNKS = 4
NY, NX, NZ = 8, 4, 8
SLAB = 32
HALF = SLAB // 2

S_CORE, S_HALF, S_RING, S_B, S_C, S_D, S_E, S_QD, S_QX, S_QZ = range(10)


def kernel(
    nc,
    cells,
    lists,
    lists_row,
    offsets,
    g,
    left,
    right,
    out,
    own,
    other,
    red,
    slab,
    bsend,
    arrived,
    csend,
    block,
    done,
    rows,
    esend,
    home_in,
    lv,
    rv,
    acc,
    sq,
    sq_d,
    sq_x,
    sq_z,
    to_column,
    slot_shard,
    back_slot,
    home,
    sem_in,
    core_r,
    ring_r,
    send_sem,
    recv_sem,
):
    per_shard = g.shape[0]
    width = g.shape[-1] // nc
    edge = g.shape[-1]
    area = edge * edge
    n_dp, n_mp = 2 * NY, NX * NZ
    R_B, R_C, R_D, R_E, R_Q = 0, nc, 2 * nc, 3 * nc, 4 * nc
    dp = lax.axis_index("dp")
    mp = lax.axis_index("mp")
    y, core = dp // 2, dp % 2
    x, z = mp // NZ, mp % NZ
    mate = {"dp": y * 2 + (1 - core)}
    y_to = [{"dp": ((y + NY - 1) % NY) * 2 + core}, {"dp": ((y + 1) % NY) * 2 + core}]

    def dp_to(o):
        return {"dp": (dp + o) % n_dp}

    def mp_to(o):
        return {"mp": (mp + o) % n_mp}

    def x_to(o):
        return {"mp": ((x + o) % NX) * NZ + z}

    def z_to(o):
        return {"mp": x * NZ + (z + o) % NZ}

    def cols(c):
        return pl.ds(c * width, width)

    def copy(src, dst, ss, rs, dev):
        return pltpu.make_async_remote_copy(
            src_ref=src, dst_ref=dst, send_sem=ss, recv_sem=rs, device_id=dev, device_id_type=MESH
        )

    def send(*args):
        copy(*args).start()

    def received(dst, rs):
        copy(dst, dst, send_sem.at[0], rs, mate).wait_recv()

    def all_sent(src, ss):
        copy(src, src, ss, recv_sem.at[0], mate).wait_send()

    loads = []
    for c in range(nc):
        load = pltpu.make_async_copy(g.at[:, :, core, :, cols(c)], own.at[c], sem_in.at[c])
        load.start()
        loads.append(load)
    load_r = pltpu.make_async_copy(right, rv, sem_in.at[nc])
    load_r.start()
    load_l = pltpu.make_async_copy(left, lv, sem_in.at[nc + 1])
    load_l.start()

    barrier = pltpu.get_barrier_semaphore()

    @pl.loop(1, n_dp)
    def _(o):
        pl.semaphore_signal(barrier, inc=1, device_id=dp_to(o), device_id_type=MESH)

    @pl.loop(1, n_mp)
    def _(o):
        pl.semaphore_signal(barrier, inc=1, device_id=mp_to(o), device_id_type=MESH)

    pl.semaphore_wait(barrier, n_dp + n_mp - 2)

    for d in [4, 5, 3, 6, 2, 7, 1, 0]:
        t = (y + d) % NY
        for c in range(nc):
            send(g.at[:, t, 1 - core, :, cols(c)], other.at[c, :, t], send_sem.at[S_CORE], core_r.at[d], mate)

    everything = pl.ds(0, SLAB)
    part = [pl.ds(0, HALF), pl.ds(HALF, HALF)]

    def mated(c, d):
        t = (y + d) % NY
        if c == 0:
            received(other.at[:, :, t], core_r.at[d])
        return t

    def pair(c, t, r):
        return own[c, :, t, r].astype(F32) + other[c, :, t, r].astype(F32)

    def a0(c):
        loads[c].wait()
        t = mated(c, 4)
        own[c, :, t] = pair(c, t, everything).astype(BF16)
        for way in range(2):
            send(
                own.at[c, :, t, part[way]],
                red.at[c, way, 0, :, part[way]],
                send_sem.at[S_HALF],
                ring_r.at[c, way, 0],
                y_to[way],
            )

    def a_mid(c, s):
        for way in range(2):
            t = mated(c, 4 + s if way == 0 else 4 - s)
            if s == 1:
                here, rest = part[way], part[1 - way]
                received(red.at[c, way, 0, :, here], ring_r.at[c, way, 0])
                own[c, :, t, here] = (pair(c, t, here) + red[c, way, 0, :, here].astype(F32)).astype(BF16)
                own[c, :, t, rest] = pair(c, t, rest).astype(BF16)
            else:
                received(red.at[c, way, s - 1], ring_r.at[c, way, s - 1])
                own[c, :, t] = (pair(c, t, everything) + red[c, way, s - 1].astype(F32)).astype(BF16)
            send(own.at[c, :, t], red.at[c, way, s], send_sem.at[S_RING], ring_r.at[c, way, s], y_to[way])

    def squares(v):
        v = (v * v).reshape(-1, 8, v.shape[-1])
        v = jnp.sum(v, axis=0)
        return sum(v[:, i * 128 : (i + 1) * 128] for i in range(v.shape[-1] // 128))

    def a4(c):
        total = pair(c, mated(c, 0), everything)
        for way in range(2):
            received(red.at[c, way, 3], ring_r.at[c, way, 3])
            total += red[c, way, 3].astype(F32)
        total = total.astype(BF16)
        slab[c] = total
        b0(c)
        part_sq = squares(total.astype(F32))
        sq[0] = part_sq if c == 0 else sq[0] + part_sq

    def tables():
        blocks = lists.shape[0]
        position = lax.broadcasted_iota(jnp.int32, (1, blocks), 1)
        column = jnp.zeros((1, blocks), jnp.int32)
        for m in range(1, n_mp + 1):
            column += jnp.where(offsets[m] <= position, 1, 0)
        homes = []
        for i in range(per_shard):
            mine = jnp.where(lists_row[...] == mp * per_shard + i, column, 0)
            homes.append(jnp.minimum(jnp.sum(mine), n_mp - 1))
            home[i] = homes[i]
        start = offsets[mp]
        count = offsets[mp + 1] - start
        shard = []
        for k in range(n_dp):
            shard.append(lists[jnp.minimum(start + k, blocks - 1)] // per_shard)
            slot_shard[k] = shard[k]

        @pl.loop(0, n_mp)
        def _(m):
            chosen = jnp.int32(0)
            for i in range(per_shard):
                chosen = jnp.where(homes[i] == m, i, chosen)
            to_column[m] = chosen
            slot = jnp.int32(0)
            for k in range(n_dp):
                slot = jnp.where((shard[k] == m) & (k < count), k, slot)
            back_slot[m] = slot

    def b0(c):
        @pl.loop(1, n_mp)
        def _(o):
            bsend[c, o] = slab[c, to_column[(mp + o) % n_mp]]
            send(bsend.at[c, o], arrived[c].at[mp], send_sem.at[S_B], recv_sem.at[R_B + c], mp_to(o))

        arrived[c][mp] = slab[c, to_column[mp]]

    def c0(c):
        received(arrived[c].at[pl.ds(1, n_mp - 1)], recv_sem.at[R_B + c])

        @pl.loop(1, n_dp)
        def _(o):
            csend[c, o] = arrived[c][slot_shard[(dp + o) % n_dp]]
            send(csend.at[c, o], block.at[c, dp], send_sem.at[S_C], recv_sem.at[R_C + c], dp_to(o))

        block[c, dp] = arrived[c][slot_shard[dp]]

    def c1(c):
        received(block.at[c, pl.ds(1, n_dp - 1)], recv_sem.at[R_C + c])
        rows_c = block[c].reshape(edge, width)
        product = jnp.dot(rows_c, rv[cols(c), :], preferred_element_type=F32)
        acc[...] = product if c == 0 else acc[...] + product
        part_sq = squares(rows_c.astype(F32))
        sq[3] = part_sq if c == 0 else sq[3] + part_sq

    def q0():
        @pl.loop(1, n_dp)
        def _(o):
            send(sq.at[0], sq_d.at[o], send_sem.at[S_QD], recv_sem.at[R_Q], dp_to(o))

    def q1():
        total = sq[0]
        received(sq_d.at[pl.ds(1, n_dp - 1)], recv_sem.at[R_Q])
        for o in range(1, n_dp):
            total += sq_d[o]
        sq[1] = total
        for o in range(1, NX):
            send(sq.at[1], sq_x.at[o], send_sem.at[S_QX], recv_sem.at[R_Q + 1], x_to(o))

    def q2():
        total = sq[1]
        received(sq_x.at[pl.ds(1, NX - 1)], recv_sem.at[R_Q + 1])
        for o in range(1, NX):
            total += sq_x[o]
        sq[2] = total
        for o in range(1, NZ):
            send(sq.at[2], sq_z.at[o], send_sem.at[S_QZ], recv_sem.at[R_Q + 2], z_to(o))

    def q3():
        total = sq[2]
        received(sq_z.at[pl.ds(1, NZ - 1)], recv_sem.at[R_Q + 2])
        for o in range(1, NZ):
            total += sq_z[o]
        return jnp.sum(total, keepdims=True)

    for c in range(nc):
        a0(c)
    tables()
    for s in (1, 2, 3):
        for c in range(nc):
            a_mid(c, s)
    for c in range(nc):
        a4(c)
    q0()
    q1()
    for c in range(nc):
        c0(c)
        if c == 0:
            q2()
            load_r.wait()
    for c in range(nc):
        c1(c)

    load_l.wait()
    acc[...] = jnp.dot(lv[...], acc[...].astype(BF16), preferred_element_type=F32)
    precond_sq = sum(squares(acc[:, cols(c)]) for c in range(nc))
    graft = jnp.sqrt(jnp.sum(sq[3], keepdims=True) / area + epsilon) / jnp.sqrt(
        jnp.sum(precond_sq, keepdims=True) / area + epsilon
    )
    clip = max_rms / jnp.sqrt(q3() / cells + epsilon)
    scale = clip * graft

    def d0(c):
        done[c] = (scale * acc[:, cols(c)]).astype(BF16).reshape(n_dp, SLAB, width)

        @pl.loop(1, n_dp)
        def _(o):
            send(done.at[c, (dp + o) % n_dp], rows[c].at[dp], send_sem.at[S_D], recv_sem.at[R_D + c], dp_to(o))

        rows[c][dp] = done[c, dp]

    def e0(c):
        received(rows[c].at[pl.ds(1, n_dp - 1)], recv_sem.at[R_D + c])

        @pl.loop(1, n_mp)
        def _(o):
            esend[c, o] = rows[c][back_slot[(mp + o) % n_mp]]
            send(esend.at[c, o], home_in[c].at[mp], send_sem.at[S_E], recv_sem.at[R_E + c], mp_to(o))

        home_in[c][mp] = rows[c][back_slot[mp]]

    def e1(c):
        received(home_in[c].at[pl.ds(1, n_mp - 1)], recv_sem.at[R_E + c])
        for i in range(per_shard):
            out[i, :, cols(c)] = home_in[c][home[i]]

    for c in range(nc):
        d0(c)
    for c in range(nc):
        e0(c)
    for c in range(nc):
        e1(c)

    all_sent(other, send_sem.at[S_CORE])
    all_sent(red.at[:, 0, 0], send_sem.at[S_HALF])
    all_sent(red.at[:, :, pl.ds(1, 3)], send_sem.at[S_RING])
    all_sent(bsend.at[:, pl.ds(1, n_mp - 1)], send_sem.at[S_B])
    all_sent(csend.at[:, pl.ds(1, n_dp - 1)], send_sem.at[S_C])
    all_sent(csend.at[:, pl.ds(1, n_dp - 1)], send_sem.at[S_D])
    all_sent(esend.at[:, pl.ds(1, n_mp - 1)], send_sem.at[S_E])
    all_sent(sq_d.at[pl.ds(1, n_dp - 1)], send_sem.at[S_QD])
    all_sent(sq_x.at[pl.ds(1, NX - 1)], send_sem.at[S_QX])
    all_sent(sq_z.at[pl.ds(1, NZ - 1)], send_sem.at[S_QZ])


def shards(grad_partials, owner_lists, owner_offsets, left_roots, right_roots):
    _, per_shard, edge, _ = grad_partials.shape
    blocks = owner_lists.shape[0]
    nc = CHUNKS
    width = edge // nc
    n_dp, n_mp = 2 * NY, NX * NZ
    g = grad_partials.reshape(per_shard, NY, 2, SLAB, edge)
    dma = pltpu.SemaphoreType.DMA

    small = pl.BlockSpec(memory_space=pltpu.SMEM)
    vmem = pl.BlockSpec(memory_space=pltpu.VMEM)
    large = pl.BlockSpec(memory_space=pltpu.HBM)
    return pl.pallas_call(
        functools.partial(kernel, nc, blocks * edge * edge),
        out_shape=jax.ShapeDtypeStruct((per_shard, SLAB, edge), BF16),
        in_specs=[small, vmem, small, large, large, large],
        out_specs=vmem,
        scratch_shapes=[
            pltpu.VMEM((nc, per_shard, NY, SLAB, width), BF16),
            pltpu.VMEM((nc, per_shard, NY, SLAB, width), BF16),
            pltpu.VMEM((nc, 2, 4, per_shard, SLAB, width), BF16),
            pltpu.VMEM((nc, per_shard, SLAB, width), BF16),
            pltpu.VMEM((nc, n_mp, SLAB, width), BF16),
            [pltpu.VMEM((n_mp, SLAB, width), BF16)] * nc,
            pltpu.VMEM((nc, n_dp, SLAB, width), BF16),
            pltpu.VMEM((nc, n_dp, SLAB, width), BF16),
            pltpu.VMEM((nc, n_dp, SLAB, width), BF16),
            [pltpu.VMEM((n_dp, SLAB, width), BF16)] * nc,
            pltpu.VMEM((nc, n_mp, SLAB, width), BF16),
            [pltpu.VMEM((n_mp, SLAB, width), BF16)] * nc,
            pltpu.VMEM((edge, edge), BF16),
            pltpu.VMEM((edge, edge), BF16),
            pltpu.VMEM((edge, edge), F32),
            pltpu.VMEM((4, 8, 128), F32),
            pltpu.VMEM((n_dp, 8, 128), F32),
            pltpu.VMEM((NX, 8, 128), F32),
            pltpu.VMEM((NZ, 8, 128), F32),
            pltpu.SMEM((n_mp,), jnp.int32),
            pltpu.SMEM((n_dp,), jnp.int32),
            pltpu.SMEM((n_mp,), jnp.int32),
            pltpu.SMEM((per_shard,), jnp.int32),
            dma((nc + 2,)),
            dma((NY,)),
            dma((nc, 2, 4)),
            dma((10,)),
            dma((4 * nc + 3,)),
        ],
        compiler_params=pltpu.CompilerParams(
            collective_id=0, has_side_effects=True, vmem_limit_bytes=63 * 1024 * 1024
        ),
    )(owner_lists, owner_lists.reshape(1, blocks), owner_offsets, g, left_roots[0, 0], right_roots[0, 0])


def solution(mesh):
    return jax.shard_map(
        shards,
        mesh=mesh,
        in_specs=(
            P("dp", "mp", None, None),
            P(),
            P(),
            P("mp", "dp", None, None),
            P("mp", "dp", None, None),
        ),
        out_specs=P("mp", "dp", None),
        check_vma=False,
    )
```

time: 383 us -> 104 us (0.27)
  waiting for transfers between devices: 215 us -> 0 us
  Pallas kernels: 0 us -> 102 us
  blocking collectives: 101 us -> 0 us
  starting transfers between devices: 19.8 us -> 0 us
  between operations: 17 us -> 0.01 us
  matrix products: 13.6 us -> 0 us
  other arithmetic: 7.38 us -> 0 us
  local copies, waits for them, and re-layouts: 8.13 us -> 1.64 us
    pallas_call x0 -> x1, Pallas kernels: none -> 102 us  [shards(): pl.pallas_call(functools.partial(kernel, nc, blocks * edge * edge), out_s...]
    psum x1 -> x0, blocking collectives: 101 us -> none  [shards(): square_total = lax.psum(jnp.sum(slab_f * slab_f), ('dp', 'mp'))]
    all_gather x1 -> x0, waiting for transfers between devices: 99 us -> none  [shards(): lax.all_gather(summed, 'mp', axis=0, tiled=True)]
    reduce_scatter x1 -> x0, waiting for transfers between devices: 70.7 us -> none  [shards(): lax.psum_scatter(partial_blocks.astype(jnp.float32).astype(jnp.bfloat16),...]
    all_to_all x3 -> x0, waiting for transfers between devices: 45 us -> none  [the longest x1 27.7 us: shards(): lax.all_to_all(outgoing_home, 'mp', split_axis=0, concat_axis=0, tiled=True)]
    all_to_all x3 -> x0, starting transfers between devices: 19.7 us -> none  [the longest x1 7.83 us: shards(): lax.all_to_all(ordered, 'dp', split_axis=0, concat_axis=1, tiled=True)[0]]
    dot_general x4 -> x0, matrix products: 13.6 us -> none  [the longest x1 10.8 us: shards(): jnp.einsum('kb,bsc->ksc', block_pick, lax.all_gather(summed, 'mp', axis=0...]
  transfers between devices with their start and end apart: 5 -> 0, of which waited for: 4 -> 0; matrix products, arithmetic and copies ran while one was open for 1% -> 0% of each run, Pallas kernels for 0% -> 0%
where the time goes in v2:
time: 104 us
  Pallas kernels  102 us (98%)
  local copies, waits for them, and re-layouts  1.64 us (2%)
    pallas_call x1, Pallas kernels, shards(): pl.pallas_call(functools.partial(kernel, nc, blocks * edge * edge), out_s...  102 us

profile of v2, /device:TPU:1, one launch (start us, length us, event | category | flops | bytes accessed | tf_op | source)
XLA Modules:
  0.0 103.7 jit_solution(8131335420303448026)
XLA Ops:
  0.0 102.0 %shard_map.55 = bf16[7,32,512]{2,1,0:T(8,128)(2,1)} custom-call(s32[224]{0:T(256)} %lists.1, s32[1,224]{1,0:T(1,128)} %bitcast.7, s32[33]{0:T(128)} %offsets.1, bf16[7,8,2,32,512]{4,3,2,1,0:T(8,128)(2,1)} %bitcast.4, bf16[512,512]{1,0:T(8,128)(2,1)} %bitcast.5, bf16[512,512]{1,0:T(8,128)(2,1)} %bitcast.6), custom_call_target="tpu_custom_call" | custom-call | tf_op jit(solution)/shard_map/pallas_call | solution.py:354
  102.0 1.6 %copy.7 = bf16[7,32,512]{2,1,0:T(8,128)(2,1)} copy(bf16[7,32,512]{2,1,0:T(8,128)(2,1)} %shard_map.55) | data formatting | bytes 458752

commit v3 on v2

--- a/solution.py
+++ b/solution.py
@@ -17,7 +17,8 @@
 CHUNKS = 4
 NY, NX, NZ = 8, 4, 8
 SLAB = 32
-HALF = SLAB // 2
+ROW_PARTS = 2
+LAG = 4
 
 S_CORE, S_HALF, S_RING, S_B, S_C, S_D, S_E, S_QD, S_QX, S_QZ = range(10)
 
@@ -63,10 +64,12 @@
 ):
     per_shard = g.shape[0]
     width = g.shape[-1] // nc
+    piece_rows = SLAB // ROW_PARTS
+    pieces = nc * ROW_PARTS
     edge = g.shape[-1]
     area = edge * edge
     n_dp, n_mp = 2 * NY, NX * NZ
-    R_B, R_C, R_D, R_E, R_Q = 0, nc, 2 * nc, 3 * nc, 4 * nc
+    R_B, R_C, R_D, R_E, R_Q = 0, pieces, 2 * pieces, 3 * pieces, 4 * pieces
     dp = lax.axis_index("dp")
     mp = lax.axis_index("mp")
     y, core = dp // 2, dp % 2
@@ -88,6 +91,9 @@
 
     def cols(c):
         return pl.ds(c * width, width)
+
+    def of(p):
+        return p // ROW_PARTS, pl.ds(p % ROW_PARTS * piece_rows, piece_rows)
 
     def copy(src, dst, ss, rs, dev):
         return pltpu.make_async_remote_copy(
@@ -125,64 +131,66 @@
 
     pl.semaphore_wait(barrier, n_dp + n_mp - 2)
 
-    for d in [4, 5, 3, 6, 2, 7, 1, 0]:
+    def swap(d):
         t = (y + d) % NY
         for c in range(nc):
             send(g.at[:, t, 1 - core, :, cols(c)], other.at[c, :, t], send_sem.at[S_CORE], core_r.at[d], mate)
 
-    everything = pl.ds(0, SLAB)
-    part = [pl.ds(0, HALF), pl.ds(HALF, HALF)]
-
-    def mated(c, d):
+    def mated(p, d):
         t = (y + d) % NY
-        if c == 0:
+        if p == 0:
             received(other.at[:, :, t], core_r.at[d])
         return t
 
-    def pair(c, t, r):
-        return own[c, :, t, r].astype(F32) + other[c, :, t, r].astype(F32)
-
-    def a0(c):
-        loads[c].wait()
-        t = mated(c, 4)
-        own[c, :, t] = pair(c, t, everything).astype(BF16)
+    def pair(c, b, t, r):
+        return own[c, b, t, r].astype(F32) + other[c, b, t, r].astype(F32)
+
+    whole = pl.ds(0, per_shard)
+
+    def split(p):
+        half = per_shard // 2 + p % 2
+        return [pl.ds(0, half), pl.ds(half, per_shard - half)]
+
+    def a0(p):
+        c, r = of(p)
+        if p % ROW_PARTS == 0:
+            loads[c].wait()
+        t = mated(p, 4)
+        own[c, :, t, r] = pair(c, whole, t, r).astype(BF16)
         for way in range(2):
-            send(
-                own.at[c, :, t, part[way]],
-                red.at[c, way, 0, :, part[way]],
-                send_sem.at[S_HALF],
-                ring_r.at[c, way, 0],
-                y_to[way],
-            )
-
-    def a_mid(c, s):
+            b = split(p)[way]
+            send(own.at[c, b, t, r], red.at[c, way, 0, b, r], send_sem.at[S_HALF], ring_r.at[p, way, 0], y_to[way])
+
+    def a_mid(p, s):
+        c, r = of(p)
         for way in range(2):
-            t = mated(c, 4 + s if way == 0 else 4 - s)
+            t = mated(p, 4 + s if way == 0 else 4 - s)
             if s == 1:
-                here, rest = part[way], part[1 - way]
-                received(red.at[c, way, 0, :, here], ring_r.at[c, way, 0])
-                own[c, :, t, here] = (pair(c, t, here) + red[c, way, 0, :, here].astype(F32)).astype(BF16)
-                own[c, :, t, rest] = pair(c, t, rest).astype(BF16)
+                b, rest = split(p)[way], split(p)[1 - way]
+                received(red.at[c, way, 0, b, r], ring_r.at[p, way, 0])
+                own[c, b, t, r] = (pair(c, b, t, r) + red[c, way, 0, b, r].astype(F32)).astype(BF16)
+                own[c, rest, t, r] = pair(c, rest, t, r).astype(BF16)
             else:
-                received(red.at[c, way, s - 1], ring_r.at[c, way, s - 1])
-                own[c, :, t] = (pair(c, t, everything) + red[c, way, s - 1].astype(F32)).astype(BF16)
-            send(own.at[c, :, t], red.at[c, way, s], send_sem.at[S_RING], ring_r.at[c, way, s], y_to[way])
+                received(red.at[c, way, s - 1, :, r], ring_r.at[p, way, s - 1])
+                own[c, :, t, r] = (pair(c, whole, t, r) + red[c, way, s - 1, :, r].astype(F32)).astype(BF16)
+            send(own.at[c, :, t, r], red.at[c, way, s, :, r], send_sem.at[S_RING], ring_r.at[p, way, s], y_to[way])
 
     def squares(v):
         v = (v * v).reshape(-1, 8, v.shape[-1])
         v = jnp.sum(v, axis=0)
         return sum(v[:, i * 128 : (i + 1) * 128] for i in range(v.shape[-1] // 128))
 
-    def a4(c):
-        total = pair(c, mated(c, 0), everything)
+    def a4(p):
+        c, r = of(p)
+        total = pair(c, whole, mated(p, 0), r)
         for way in range(2):
-            received(red.at[c, way, 3], ring_r.at[c, way, 3])
-            total += red[c, way, 3].astype(F32)
+            received(red.at[c, way, 3, :, r], ring_r.at[p, way, 3])
+            total += red[c, way, 3, :, r].astype(F32)
         total = total.astype(BF16)
-        slab[c] = total
-        b0(c)
+        slab[c, :, r] = total
+        b0(p)
         part_sq = squares(total.astype(F32))
-        sq[0] = part_sq if c == 0 else sq[0] + part_sq
+        sq[0] = part_sq if p == 0 else sq[0] + part_sq
 
     def tables():
         blocks = lists.shape[0]
@@ -213,26 +221,32 @@
                 slot = jnp.where((shard[k] == m) & (k < count), k, slot)
             back_slot[m] = slot
 
-    def b0(c):
+    def b0(p):
+        c, r = of(p)
+
         @pl.loop(1, n_mp)
         def _(o):
-            bsend[c, o] = slab[c, to_column[(mp + o) % n_mp]]
-            send(bsend.at[c, o], arrived[c].at[mp], send_sem.at[S_B], recv_sem.at[R_B + c], mp_to(o))
-
-        arrived[c][mp] = slab[c, to_column[mp]]
-
-    def c0(c):
-        received(arrived[c].at[pl.ds(1, n_mp - 1)], recv_sem.at[R_B + c])
+            bsend[c, o, r] = slab[c, to_column[(mp + o) % n_mp], r]
+            send(bsend.at[c, o, r], arrived[p].at[mp], send_sem.at[S_B], recv_sem.at[R_B + p], mp_to(o))
+
+        arrived[p][mp] = slab[c, to_column[mp], r]
+
+    def c0(p):
+        c, r = of(p)
+        received(arrived[p].at[pl.ds(1, n_mp - 1)], recv_sem.at[R_B + p])
 
         @pl.loop(1, n_dp)
         def _(o):
-            csend[c, o] = arrived[c][slot_shard[(dp + o) % n_dp]]
-            send(csend.at[c, o], block.at[c, dp], send_sem.at[S_C], recv_sem.at[R_C + c], dp_to(o))
-
-        block[c, dp] = arrived[c][slot_shard[dp]]
-
-    def c1(c):
-        received(block.at[c, pl.ds(1, n_dp - 1)], recv_sem.at[R_C + c])
+            csend[c, o, r] = arrived[p][slot_shard[(dp + o) % n_dp]]
+            send(csend.at[c, o, r], block.at[c, dp, r], send_sem.at[S_C], recv_sem.at[R_C + p], dp_to(o))
+
+        block[c, dp, r] = arrived[p][slot_shard[dp]]
+
+    def c1(p):
+        c, r = of(p)
+        received(block.at[c, pl.ds(1, n_dp - 1), r], recv_sem.at[R_C + p])
+        if (p + 1) % ROW_PARTS:
+            return
         rows_c = block[c].reshape(edge, width)
         product = jnp.dot(rows_c, rv[cols(c), :], preferred_element_type=F32)
         acc[...] = product if c == 0 else acc[...] + product
@@ -269,23 +283,32 @@
             total += sq_z[o]
         return jnp.sum(total, keepdims=True)
 
-    for c in range(nc):
-        a0(c)
-    tables()
-    for s in (1, 2, 3):
-        for c in range(nc):
-            a_mid(c, s)
-    for c in range(nc):
-        a4(c)
+    for d in (4, 5, 3):
+        swap(d)
+    stages = [a0] + [functools.partial(a_mid, s=s) for s in (1, 2, 3)] + [a4]
+    last = pieces - 1
+    for turn in range(len(stages) + last // LAG):
+        if 1 <= turn <= 3:
+            for d in ((6, 2), (7, 1), (0,))[turn - 1]:
+                swap(d)
+        for p in range(pieces):
+            n = turn - p // LAG
+            if 0 <= n < len(stages):
+                stages[n](p)
+        if turn == 0:
+            tables()
     q0()
     q1()
-    for c in range(nc):
-        c0(c)
-        if c == 0:
+    for p in range(pieces):
+        c0(p)
+        if p == 0:
+            load_r.wait()
+        if p == 1:
             q2()
-            load_r.wait()
-    for c in range(nc):
-        c1(c)
+        if p >= 2:
+            c1(p - 2)
+    c1(last - 1)
+    c1(last)
 
     load_l.wait()
     acc[...] = jnp.dot(lv[...], acc[...].astype(BF16), preferred_element_type=F32)
@@ -296,36 +319,40 @@
     clip = max_rms / jnp.sqrt(q3() / cells + epsilon)
     scale = clip * graft
 
-    def d0(c):
-        done[c] = (scale * acc[:, cols(c)]).astype(BF16).reshape(n_dp, SLAB, width)
+    def d0(p):
+        c, r = of(p)
+        if p % ROW_PARTS == 0:
+            done[c] = (scale * acc[:, cols(c)]).astype(BF16).reshape(n_dp, SLAB, width)
 
         @pl.loop(1, n_dp)
         def _(o):
-            send(done.at[c, (dp + o) % n_dp], rows[c].at[dp], send_sem.at[S_D], recv_sem.at[R_D + c], dp_to(o))
-
-        rows[c][dp] = done[c, dp]
-
-    def e0(c):
-        received(rows[c].at[pl.ds(1, n_dp - 1)], recv_sem.at[R_D + c])
+            send(done.at[c, (dp + o) % n_dp, r], rows[p].at[dp], send_sem.at[S_D], recv_sem.at[R_D + p], dp_to(o))
+
+        rows[p][dp] = done[c, dp, r]
+
+    def e0(p):
+        c, r = of(p)
+        received(rows[p].at[pl.ds(1, n_dp - 1)], recv_sem.at[R_D + p])
 
         @pl.loop(1, n_mp)
         def _(o):
-            esend[c, o] = rows[c][back_slot[(mp + o) % n_mp]]
-            send(esend.at[c, o], home_in[c].at[mp], send_sem.at[S_E], recv_sem.at[R_E + c], mp_to(o))
-
-        home_in[c][mp] = rows[c][back_slot[mp]]
-
-    def e1(c):
-        received(home_in[c].at[pl.ds(1, n_mp - 1)], recv_sem.at[R_E + c])
+            esend[c, o, r] = rows[p][back_slot[(mp + o) % n_mp]]
+            send(esend.at[c, o, r], home_in[p].at[mp], send_sem.at[S_E], recv_sem.at[R_E + p], mp_to(o))
+
+        home_in[p][mp] = rows[p][back_slot[mp]]
+
+    def e1(p):
+        c, r = of(p)
+        received(home_in[p].at[pl.ds(1, n_mp - 1)], recv_sem.at[R_E + p])
         for i in range(per_shard):
-            out[i, :, cols(c)] = home_in[c][home[i]]
-
-    for c in range(nc):
-        d0(c)
-    for c in range(nc):
-        e0(c)
-    for c in range(nc):
-        e1(c)
+            out[i, r, cols(c)] = home_in[p][home[i]]
+
+    for p in range(pieces):
+        d0(p)
+    for p in range(pieces):
+        e0(p)
+    for p in range(pieces):
+        e1(p)
 
     all_sent(other, send_sem.at[S_CORE])
     all_sent(red.at[:, 0, 0], send_sem.at[S_HALF])
@@ -344,6 +371,8 @@
     blocks = owner_lists.shape[0]
     nc = CHUNKS
     width = edge // nc
+    piece_rows = SLAB // ROW_PARTS
+    pieces = nc * ROW_PARTS
     n_dp, n_mp = 2 * NY, NX * NZ
     g = grad_partials.reshape(per_shard, NY, 2, SLAB, edge)
     dma = pltpu.SemaphoreType.DMA
@@ -362,13 +391,13 @@
             pltpu.VMEM((nc, 2, 4, per_shard, SLAB, width), BF16),
             pltpu.VMEM((nc, per_shard, SLAB, width), BF16),
             pltpu.VMEM((nc, n_mp, SLAB, width), BF16),
-            [pltpu.VMEM((n_mp, SLAB, width), BF16)] * nc,
+            [pltpu.VMEM((n_mp, piece_rows, width), BF16)] * pieces,
             pltpu.VMEM((nc, n_dp, SLAB, width), BF16),
             pltpu.VMEM((nc, n_dp, SLAB, width), BF16),
             pltpu.VMEM((nc, n_dp, SLAB, width), BF16),
-            [pltpu.VMEM((n_dp, SLAB, width), BF16)] * nc,
+            [pltpu.VMEM((n_dp, piece_rows, width), BF16)] * pieces,
             pltpu.VMEM((nc, n_mp, SLAB, width), BF16),
-            [pltpu.VMEM((n_mp, SLAB, width), BF16)] * nc,
+            [pltpu.VMEM((n_mp, piece_rows, width), BF16)] * pieces,
             pltpu.VMEM((edge, edge), BF16),
             pltpu.VMEM((edge, edge), BF16),
             pltpu.VMEM((edge, edge), F32),
@@ -382,9 +411,9 @@
             pltpu.SMEM((per_shard,), jnp.int32),
             dma((nc + 2,)),
             dma((NY,)),
-            dma((nc, 2, 4)),
+            dma((pieces, 2, 4)),
             dma((10,)),
-            dma((4 * nc + 3,)),
+            dma((4 * pieces + 3,)),
         ],
         compiler_params=pltpu.CompilerParams(
             collective_id=0, has_side_effects=True, vmem_limit_bytes=63 * 1024 * 1024

time: 104 us -> 101 us (0.971)
  Pallas kernels: 102 us -> 99.2 us
    pallas_call x1, Pallas kernels: 102 us -> 99.2 us  [shards(): pl.pallas_call(functools.partial(kernel, nc, blocks * edge * edge), out_s...]
where the time goes in v3:
time: 101 us
  Pallas kernels  99.2 us (98%)
  local copies, waits for them, and re-layouts  1.64 us (2%)
    pallas_call x1, Pallas kernels, shards(): pl.pallas_call(functools.partial(kernel, nc, blocks * edge * edge), out_s...  99.2 us

profile of v3, /device:TPU:1, one launch (start us, length us, event | category | flops | bytes accessed | tf_op | source)
XLA Modules:
  0.0 100.8 jit_solution(12417911509356474244)
XLA Ops:
  0.0 99.2 %shard_map.55 = bf16[7,32,512]{2,1,0:T(8,128)(2,1)} custom-call(s32[224]{0:T(256)} %lists.1, s32[1,224]{1,0:T(1,128)} %bitcast.7, s32[33]{0:T(128)} %offsets.1, bf16[7,8,2,32,512]{4,3,2,1,0:T(8,128)(2,1)} %bitcast.4, bf16[512,512]{1,0:T(8,128)(2,1)} %bitcast.5, bf16[512,512]{1,0:T(8,128)(2,1)} %bitcast.6), custom_call_target="tpu_custom_call" | custom-call | tf_op jit(solution)/shard_map/pallas_call | solution.py:383
  99.2 1.6 %copy.7 = bf16[7,32,512]{2,1,0:T(8,128)(2,1)} copy(bf16[7,32,512]{2,1,0:T(8,128)(2,1)} %shard_map.55) | data formatting | bytes 458752

commit v4 on v3

--- a/solution.py
+++ b/solution.py
@@ -18,7 +18,7 @@
 NY, NX, NZ = 8, 4, 8
 SLAB = 32
 ROW_PARTS = 2
-LAG = 4
+LAG = 8
 
 S_CORE, S_HALF, S_RING, S_B, S_C, S_D, S_E, S_QD, S_QX, S_QZ = range(10)
 
@@ -61,6 +61,7 @@
     ring_r,
     send_sem,
     recv_sem,
+    entered,
 ):
     per_shard = g.shape[0]
     width = g.shape[-1] // nc
@@ -80,8 +81,14 @@
     def dp_to(o):
         return {"dp": (dp + o) % n_dp}
 
-    def mp_to(o):
-        return {"mp": (mp + o) % n_mp}
+    def around(k):
+        return 4 + k // 2 - (k % 2) * k
+
+    def mp_at(o):
+        return ((x + NX - 1 - o % NX) % NX) * NZ + (z + around(o // NX)) % NZ
+
+    def dp_at(o):
+        return ((y + around(o // 2)) % NY) * 2 + (core + 1 - o % 2) % 2
 
     def x_to(o):
         return {"mp": ((x + o) % NX) * NZ + z}
@@ -120,16 +127,23 @@
     load_l.start()
 
     barrier = pltpu.get_barrier_semaphore()
-
-    @pl.loop(1, n_dp)
-    def _(o):
-        pl.semaphore_signal(barrier, inc=1, device_id=dp_to(o), device_id_type=MESH)
-
-    @pl.loop(1, n_mp)
-    def _(o):
-        pl.semaphore_signal(barrier, inc=1, device_id=mp_to(o), device_id_type=MESH)
-
-    pl.semaphore_wait(barrier, n_dp + n_mp - 2)
+    rank = z * NX + x
+
+    def ranked(r):
+        return {"mp": (r % NX) * NZ + r // NX}
+
+    for near in (*y_to, mate):
+        pl.semaphore_signal(barrier, inc=1, device_id=near, device_id_type=MESH)
+
+    @pl.loop(rank + 1, n_mp)
+    def _(r):
+        pl.semaphore_signal(barrier, inc=1, device_id=ranked(r), device_id_type=MESH)
+
+    pl.semaphore_wait(barrier, 3 + rank)
+
+    @pl.loop(0, rank)
+    def _(r):
+        pl.semaphore_signal(entered, inc=1, device_id=ranked(r), device_id_type=MESH)
 
     def swap(d):
         t = (y + d) % NY
@@ -224,10 +238,11 @@
     def b0(p):
         c, r = of(p)
 
-        @pl.loop(1, n_mp)
+        @pl.loop(0, n_mp - 1)
         def _(o):
-            bsend[c, o, r] = slab[c, to_column[(mp + o) % n_mp], r]
-            send(bsend.at[c, o, r], arrived[p].at[mp], send_sem.at[S_B], recv_sem.at[R_B + p], mp_to(o))
+            to = mp_at(o)
+            bsend[c, o, r] = slab[c, to_column[to], r]
+            send(bsend.at[c, o, r], arrived[p].at[mp], send_sem.at[S_B], recv_sem.at[R_B + p], {"mp": to})
 
         arrived[p][mp] = slab[c, to_column[mp], r]
 
@@ -235,10 +250,11 @@
         c, r = of(p)
         received(arrived[p].at[pl.ds(1, n_mp - 1)], recv_sem.at[R_B + p])
 
-        @pl.loop(1, n_dp)
+        @pl.loop(0, n_dp - 1)
         def _(o):
-            csend[c, o, r] = arrived[p][slot_shard[(dp + o) % n_dp]]
-            send(csend.at[c, o, r], block.at[c, dp, r], send_sem.at[S_C], recv_sem.at[R_C + p], dp_to(o))
+            to = dp_at(o)
+            csend[c, o, r] = arrived[p][slot_shard[to]]
+            send(csend.at[c, o, r], block.at[c, dp, r], send_sem.at[S_C], recv_sem.at[R_C + p], {"dp": to})
 
         block[c, dp, r] = arrived[p][slot_shard[dp]]
 
@@ -288,6 +304,12 @@
     stages = [a0] + [functools.partial(a_mid, s=s) for s in (1, 2, 3)] + [a4]
     last = pieces - 1
     for turn in range(len(stages) + last // LAG):
+        if turn == 4:
+
+            @pl.when(rank < n_mp - 1)
+            def _():
+                pl.semaphore_wait(entered, n_mp - 1 - rank)
+
         if 1 <= turn <= 3:
             for d in ((6, 2), (7, 1), (0,))[turn - 1]:
                 swap(d)
@@ -324,9 +346,10 @@
         if p % ROW_PARTS == 0:
             done[c] = (scale * acc[:, cols(c)]).astype(BF16).reshape(n_dp, SLAB, width)
 
-        @pl.loop(1, n_dp)
+        @pl.loop(0, n_dp - 1)
         def _(o):
-            send(done.at[c, (dp + o) % n_dp, r], rows[p].at[dp], send_sem.at[S_D], recv_sem.at[R_D + p], dp_to(o))
+            to = dp_at(o)
+            send(done.at[c, to, r], rows[p].at[dp], send_sem.at[S_D], recv_sem.at[R_D + p], {"dp": to})
 
         rows[p][dp] = done[c, dp, r]
 
@@ -334,10 +357,11 @@
         c, r = of(p)
         received(rows[p].at[pl.ds(1, n_dp - 1)], recv_sem.at[R_D + p])
 
-        @pl.loop(1, n_mp)
+        @pl.loop(0, n_mp - 1)
         def _(o):
-            esend[c, o, r] = rows[p][back_slot[(mp + o) % n_mp]]
-            send(esend.at[c, o, r], home_in[p].at[mp], send_sem.at[S_E], recv_sem.at[R_E + p], mp_to(o))
+            to = mp_at(o)
+            esend[c, o, r] = rows[p][back_slot[to]]
+            send(esend.at[c, o, r], home_in[p].at[mp], send_sem.at[S_E], recv_sem.at[R_E + p], {"mp": to})
 
         home_in[p][mp] = rows[p][back_slot[mp]]
 
@@ -414,6 +438,7 @@
             dma((pieces, 2, 4)),
             dma((10,)),
             dma((4 * pieces + 3,)),
+            pltpu.SemaphoreType.REGULAR,
         ],
         compiler_params=pltpu.CompilerParams(
             collective_id=0, has_side_effects=True, vmem_limit_bytes=63 * 1024 * 1024

time: 101 us -> 97.8 us (0.968)
  Pallas kernels: 99.2 us -> 95.9 us
    pallas_call x1, Pallas kernels: 99.2 us -> 95.9 us  [shards(): pl.pallas_call(functools.partial(kernel, nc, blocks * edge * edge), out_s...]
where the time goes in v4:
time: 97.8 us; the launch traced here: 97.6 us
  Pallas kernels  95.9 us (98%)
  local copies, waits for them, and re-layouts  1.64 us (2%)
    pallas_call x1, Pallas kernels, shards(): pl.pallas_call(functools.partial(kernel, nc, blocks * edge * edge), out_s...  95.9 us

profile of v4, /device:TPU:1, one launch (start us, length us, event | category | flops | bytes accessed | tf_op | source)
XLA Modules:
  0.0 97.6 jit_solution(5887157466777498376)
XLA Ops:
  0.0 95.9 %shard_map.55 = bf16[7,32,512]{2,1,0:T(8,128)(2,1)} custom-call(s32[224]{0:T(256)} %lists.1, s32[1,224]{1,0:T(1,128)} %bitcast.7, s32[33]{0:T(128)} %offsets.1, bf16[7,8,2,32,512]{4,3,2,1,0:T(8,128)(2,1)} %bitcast.4, bf16[512,512]{1,0:T(8,128)(2,1)} %bitcast.5, bf16[512,512]{1,0:T(8,128)(2,1)} %bitcast.6), custom_call_target="tpu_custom_call" | custom-call | tf_op jit(solution)/shard_map/pallas_call | solution.py:407
  95.9 1.6 %copy.7 = bf16[7,32,512]{2,1,0:T(8,128)(2,1)} copy(bf16[7,32,512]{2,1,0:T(8,128)(2,1)} %shard_map.55) | data formatting | bytes 458752

commit v5 on v4

--- a/solution.py
+++ b/solution.py
@@ -173,21 +173,20 @@
         own[c, :, t, r] = pair(c, whole, t, r).astype(BF16)
         for way in range(2):
             b = split(p)[way]
-            send(own.at[c, b, t, r], red.at[c, way, 0, b, r], send_sem.at[S_HALF], ring_r.at[p, way, 0], y_to[way])
+            send(own.at[c, b, t, r], red.at[c, way, 0, b, r], send_sem.at[S_HALF], ring_r.at[p, 0], y_to[way])
 
     def a_mid(p, s):
         c, r = of(p)
+        received(red.at[c, 0, 0, :, r] if s == 1 else red.at[c, :, s - 1, :, r], ring_r.at[p, s - 1])
         for way in range(2):
             t = mated(p, 4 + s if way == 0 else 4 - s)
             if s == 1:
                 b, rest = split(p)[way], split(p)[1 - way]
-                received(red.at[c, way, 0, b, r], ring_r.at[p, way, 0])
                 own[c, b, t, r] = (pair(c, b, t, r) + red[c, way, 0, b, r].astype(F32)).astype(BF16)
                 own[c, rest, t, r] = pair(c, rest, t, r).astype(BF16)
             else:
-                received(red.at[c, way, s - 1, :, r], ring_r.at[p, way, s - 1])
                 own[c, :, t, r] = (pair(c, whole, t, r) + red[c, way, s - 1, :, r].astype(F32)).astype(BF16)
-            send(own.at[c, :, t, r], red.at[c, way, s, :, r], send_sem.at[S_RING], ring_r.at[p, way, s], y_to[way])
+            send(own.at[c, :, t, r], red.at[c, way, s, :, r], send_sem.at[S_RING], ring_r.at[p, s], y_to[way])
 
     def squares(v):
         v = (v * v).reshape(-1, 8, v.shape[-1])
@@ -197,8 +196,8 @@
     def a4(p):
         c, r = of(p)
         total = pair(c, whole, mated(p, 0), r)
+        received(red.at[c, :, 3, :, r], ring_r.at[p, 3])
         for way in range(2):
-            received(red.at[c, way, 3, :, r], ring_r.at[p, way, 3])
             total += red[c, way, 3, :, r].astype(F32)
         total = total.astype(BF16)
         slab[c, :, r] = total
@@ -435,7 +434,7 @@
             pltpu.SMEM((per_shard,), jnp.int32),
             dma((nc + 2,)),
             dma((NY,)),
-            dma((pieces, 2, 4)),
+            dma((pieces, 4)),
             dma((10,)),
             dma((4 * pieces + 3,)),
             pltpu.SemaphoreType.REGULAR,

time: 97.8 us -> 97.9 us (level)
  no operation moved by 1% of the time
where the time goes in v5:
time: 97.9 us; the launch traced here: 97.7 us
  Pallas kernels  96 us (98%)
  local copies, waits for them, and re-layouts  1.64 us (2%)
    pallas_call x1, Pallas kernels, shards(): pl.pallas_call(functools.partial(kernel, nc, blocks * edge * edge), out_s...  96 us

profile of v5, /device:TPU:1, one launch (start us, length us, event | category | flops | bytes accessed | tf_op | source)
XLA Modules:
  0.0 97.7 jit_solution(3879974435169335748)
XLA Ops:
  0.0 96.0 %shard_map.55 = bf16[7,32,512]{2,1,0:T(8,128)(2,1)} custom-call(s32[224]{0:T(256)} %lists.1, s32[1,224]{1,0:T(1,128)} %bitcast.7, s32[33]{0:T(128)} %offsets.1, bf16[7,8,2,32,512]{4,3,2,1,0:T(8,128)(2,1)} %bitcast.4, bf16[512,512]{1,0:T(8,128)(2,1)} %bitcast.5, bf16[512,512]{1,0:T(8,128)(2,1)} %bitcast.6), custom_call_target="tpu_custom_call" | custom-call | tf_op jit(solution)/shard_map/pallas_call | solution.py:406
  96.0 1.6 %copy.7 = bf16[7,32,512]{2,1,0:T(8,128)(2,1)} copy(bf16[7,32,512]{2,1,0:T(8,128)(2,1)} %shard_map.55) | data formatting | bytes 458752
